TPU v7x, 32 devices: a whole 2x2x4 slice. The times are simulated.
32 devices in a mesh: wide: 16 (over z, y, x), narrow: 2 (over core).
Axes of the slice: x: 2, y: 2, z: 4, core: 2. Of those that a mesh axis runs over, the one named last changes fastest.
Arguments:
- output_gradient: bfloat16 [1024, 16384], P('wide', 'narrow'), may hold values from -6 to 6
- packed_weight_codes: int32 [49152, 8192], P('wide', 'narrow'), may hold values from 0 to 255
- group_zero_offsets: int32 [384, 16384], P('wide', 'narrow'), may hold values from 0 to 15
- group_scale_table: float32 [384, 16384], P('wide', 'narrow'), may hold values from 0.0004 to 0.004
- channel_aware_scale: float32 [49152], P('wide'), may hold values from 0.5 to 2
- adapter_down_matrix: bfloat16 [49152, 16], P('wide'), may hold values from -1.5 to 1.5
- adapter_up_matrix: bfloat16 [16, 16384], P(None, 'narrow'), may hold values from -0.046875 to 0.046875
Outputs:
- grad_input: bfloat16 [1024, 49152], P('narrow', 'wide')
Inputs may be any that keep to these rules, and one draw needn't show every extreme that they name: `packed_weight_codes`: word column 128 * b + i holds the code of output column 2 * 128 * b + i in its value modulo 16 and that of column 2 * 128 * b + 128 + i in its value divided by 16.
All inputs are finite; a program needn't handle non-finite values.
Results may differ from a plain program's by a relative error of at most 0.0048.
Values may be sent and summed in bfloat16 or wider, within the bound.
A program may use at most 512 MiB of HBM per device.

v0:
```python
import jax
import jax.numpy as jnp
from jax import lax
from jax.sharding import PartitionSpec as P

GROUP = 128
HALF = 128


adapter_gain = 0.5


def unpack(words, zero_rows, scale_rows):
    rows, half_cols = words.shape
    low_codes = words % 16
    high_codes = words // 16
    blocks = half_cols // HALF
    codes = jnp.stack(
        [low_codes.reshape(rows, blocks, HALF), high_codes.reshape(rows, blocks, HALF)], axis=2
    ).reshape(rows, 2 * half_cols)
    groups = rows // GROUP
    shifted = (codes.reshape(groups, GROUP, 2 * half_cols) - zero_rows[:, None, :]).astype(
        jnp.float32
    )
    return (shifted * scale_rows[:, None, :]).reshape(rows, 2 * half_cols).astype(jnp.bfloat16)


def shards(
    output_gradient,
    packed_weight_codes,
    group_zero_offsets,
    group_scale_table,
    channel_aware_scale,
    adapter_down_matrix,
    adapter_up_matrix,
):
    weight = unpack(packed_weight_codes, group_zero_offsets, group_scale_table)
    dequantized_down = adapter_down_matrix.astype(jnp.float32)
    collected_rows = lax.all_gather(output_gradient, "wide", axis=0, tiled=True)
    adapter_inner_piece = jnp.einsum(
        "ch,jh->cj", collected_rows, adapter_up_matrix, preferred_element_type=jnp.float32
    )
    total = collected_rows.shape[0]
    own_count = total // lax.axis_size("narrow")
    adapter_inner_total = lax.psum(adapter_inner_piece, "narrow")
    local_owned_rows = lax.psum_scatter(
        jnp.einsum("td,kd->tk", collected_rows, weight, preferred_element_type=jnp.float32)
        / channel_aware_scale[None, :],
        "narrow",
        scatter_dimension=0,
        tiled=True,
    )
    own_start = lax.axis_index("narrow") * own_count
    own_inner = lax.dynamic_slice_in_dim(adapter_inner_total, own_start, own_count, 0)
    local_owned_rows = local_owned_rows + adapter_gain * jnp.dot(
        own_inner, dequantized_down.T, precision=lax.Precision.HIGHEST
    )
    return local_owned_rows.astype(jnp.bfloat16)


def solution(mesh):
    placed = (
        P("wide", "narrow"),
        P("wide", "narrow"),
        P("wide", "narrow"),
        P("wide", "narrow"),
        P("wide"),
        P("wide", None),
        P(None, "narrow"),
    )
    return jax.shard_map(
        shards, mesh=mesh, in_specs=placed, out_specs=P("narrow", "wide"), check_vma=False
    )
```

profile of v0, /device:TPU:0, one launch (start us, length us, event | category | flops | bytes accessed | tf_op | source)
XLA Modules:
  0.0 523.2 jit_solution(10566105741058044407)
XLA Ops:
  6.5 0.0 copy-start
  6.5 0.0 all-gather.2.cloned.1.call-start
  6.5 0.7 all-gather.2.cloned.1.call-update
  7.3 0.0 all-reduce.2.cloned.1.call-start
  7.3 50.3 %add_select_fusion.1 = (s32[3072,4096]{1,0:T(8,128)}, s32[3072,4096]{1,0:T(8,128)}) fusion(s32[3072,4096]{1,0:T(8,128)} %param.8), kind=kLoop, calls=%fused_computation.7 | loop fusion | flops 239075328 | bytes 150994944 | tf_op jit(solution)/shard_map/jit(remainder)/select_n | solution.py:15
  57.6 48.9 %copy.10 = s32[3072,4096]{0,1:T(8,128)} copy(s32[3072,4096]{1,0:T(8,128)} %get-tuple-element.5) | data formatting | bytes 100663296 | tf_op jit(solution)/shard_map/jit(remainder)/select_n | solution.py:15
  106.4 0.0 copy-start.2
  106.4 0.0 copy-start.3
  106.4 49.1 %copy.11 = s32[3072,4096]{0,1:T(8,128)} copy(s32[3072,4096]{1,0:T(8,128)} %get-tuple-element.6) | data formatting | bytes 100663296 | tf_op jit(solution)/shard_map/jit(floor_divide)/jit(_where)/select_n | solution.py:16
  155.5 0.0 copy-done.2
  155.5 2.7 copy.12
  158.2 0.0 copy-done.3
  158.2 2.7 copy.13
  160.9 65.3 %pad_add_fusion = s32[3072,32,2,128]{0,3,2,1:T(8,128)} fusion(s32[3072,32,1,128]{0,3,2,1:T(8,128)} %bitcast.28, s32[3072,32,1,128]{0,3,2,1:T(8,128)} %bitcast.27), kind=kLoop, calls=%fused_computation.4 | loop fusion | flops 25165824 | bytes 201326592 | tf_op jit(solution)/shard_map/stack | solution.py:18
  226.2 0.0 copy-start.1
  226.2 34.2 %sub.18 = s32[24,128,8192]{1,0,2:T(8,128)} broadcast(s32[24,8192]{0,1:T(8,128)} %copy.12), dimensions={0,2} | broadcast | bytes 101449728 | tf_op jit(solution)/shard_map/sub | solution.py:22
  260.4 0.0 copy-done.1
  260.4 31.7 %mul.20 = f32[24,128,8192]{1,0,2:T(8,128)} broadcast(f32[24,8192]{0,1:T(8,128)S(1)} %copy-done.1), dimensions={0,2} | broadcast | bytes 101449728 | tf_op jit(solution)/shard_map/mul | solution.py:25
  292.1 0.0 copy-start.5
  292.1 118.8 %fusion = bf16[3072,8192]{0,1:T(8,128)(2,1)} fusion(f32[1024,8,24,128]{3,2,1,0:T(8,128)} %bitcast.9, s32[1024,8,24,128]{3,2,1,0:T(8,128)} %bitcast.5, s32[3072,32,2,128]{0,3,2,1:T(8,128)} %pad_add_fusion), kind=kLoop, calls=%fused_computation.1 | loop fusion | flops 100663296 | bytes 352321536 | tf_op jit(solution)/shard_map/convert_element_type | solution.py:25
  410.8 0.0 all-gather.2.cloned.1.call-done
  410.8 0.0 copy-done
  410.8 9.0 %fusion.6 = f32[1024,16]{1,0:T(8,128)} fusion(bf16[1024,8192]{1,0:T(8,128)(2,1)} %all-gather.2.cloned.1.call-done, bf16[16,8192]{1,0:T(8,128)(2,1)S(1)} %copy-done), kind=kOutput, calls=%fused_computation.17 | convolution fusion | flops 268435456 | bytes 17104896 | tf_op jit(solution)/shard_map/ch,jh->cj/dot_general | solution.py:40
  419.9 0.0 all-reduce.2.cloned.1.call-update
  419.9 0.0 copy-start.4
  419.9 0.0 reduce-scatter.2.cloned.1.call-start
  420.0 0.0 copy-done.5
  420.0 63.1 %divide_bitcast_fusion = f32[1024,3072]{0,1:T(8,128)} fusion(bf16[3072,8192]{0,1:T(8,128)(2,1)} %fusion, bf16[1024,8192]{1,0:T(8,128)(2,1)} %all-gather.2.cloned.1.call-done, f32[3072]{0:T(1024)S(1)} %copy-done.5), kind=kOutput, calls=%fused_computation.13 | convolution fusion | flops 51542753280 | bytes 79704064 | tf_op jit(solution)/shard_map/td,kd->tk/dot_general | solution.py:47
  483.1 0.0 reduce-scatter.2.cloned.1.call-update
  483.1 0.0 all-reduce.2.cloned.1.call-done
  483.1 25.4 %reduce-scatter.2.cloned.1.call-done = f32[512,3072]{0,1:T(8,128)} async-done(((f32[1024,3072]{0,1:T(8,128)}), f32[512,3072]{0,1:T(8,128)}) %reduce-scatter.2.cloned.1.call-update) | async-done | bytes 6291472 | tf_op jit(solution)/shard_map/reduce_scatter | solution.py:46
  508.6 0.0 copy-done.4
  508.6 5.0 add_convert_fusion
  513.6 3.0 copy.15
Async XLA Ops:
  6.5 404.3 %copy-start = (bf16[16,8192]{1,0:T(8,128)(2,1)S(1)}, bf16[16,8192]{1,0:T(8,128)(2,1)}, u32[]{:S(2)}) copy-start(bf16[16,8192]{1,0:T(8,128)(2,1)} %param.13) | copy-start | bytes 786436
  6.5 404.3 %all-gather.2.cloned.1.call-start = ((), (), s32[]{:S(2)}) async-start(), calls=%async_computation.1 | async-start | bytes 17825792 | tf_op jit(solution)/shard_map/all_gather | solution.py:39
  7.3 475.9 %all-reduce.2.cloned.1.call-start = ((), (), s32[]{:S(2)}) async-start(), calls=%async_computation.3 | async-start | bytes 1048576 | tf_op jit(solution)/shard_map/psum | solution.py:45
  106.4 49.1 %copy-start.2 = (s32[24,8192]{1,0:T(8,128)S(1)}, s32[24,8192]{1,0:T(8,128)}, u32[]{:S(2)}) copy-start(s32[24,8192]{1,0:T(8,128)} %param.9) | copy-start | bytes 2359300
  106.4 51.8 %copy-start.3 = (f32[24,8192]{1,0:T(8,128)S(1)}, f32[24,8192]{1,0:T(8,128)}, u32[]{:S(2)}) copy-start(f32[24,8192]{1,0:T(8,128)} %param.10) | copy-start | bytes 2359300
  226.2 34.2 %copy-start.1 = (f32[24,8192]{0,1:T(8,128)S(1)}, f32[24,8192]{0,1:T(8,128)}, u32[]{:S(2)}) copy-start(f32[24,8192]{0,1:T(8,128)} %copy.13) | copy-start | bytes 2359300
  292.1 127.9 %copy-start.5 = (f32[3072]{0:T(1024)S(1)}, f32[3072]{0:T(1024)}, u32[]{:S(2)}) copy-start(f32[3072]{0:T(1024)} %param.11) | copy-start | bytes 36868
  419.9 88.7 %copy-start.4 = (bf16[3072,16]{0,1:T(8,128)(2,1)S(1)}, bf16[3072,16]{0,1:T(8,128)(2,1)}, u32[]{:S(2)}) copy-start(bf16[3072,16]{0,1:T(8,128)(2,1)} %param.12) | copy-start | bytes 294916
  419.9 88.6 %reduce-scatter.2.cloned.1.call-start = ((), (), s32[]{:S(2)}) async-start(), calls=%async_computation.2 | async-start | bytes 18874368 | tf_op jit(solution)/shard_map/reduce_scatter | solution.py:46
Sparse Core Ops, SparseCore 0:
  10.1 194.3 all-gather.1
  420.0 22.5 all-reduce.1
  483.2 25.3 reduce-scatter.1
where the time goes:
time: 524 us; the launch traced here: 523 us
  other arithmetic  234 us (45%)
  local copies, waits for them, and re-layouts  172 us (33%)
  matrix products  77.2 us (15%)
  waiting for transfers between devices  26.2 us (5%)
  between operations  13.2 us (3%)
    convert_element_type x1, other arithmetic, unpack(): (shifted * scale_rows[:, None, :]).reshape(rows, 2 * half_cols)  119 us
    another operation x1, other arithmetic, unpack(): jnp.stack([low_codes.reshape(rows, blocks, HALF), high_codes.reshape(rows...  65.3 us
    dot_general x1, matrix products, shards(): jnp.einsum('td,kd->tk', collected_rows, weight, preferred_element_type=jn...  63.1 us
    select_n x1, other arithmetic, unpack(): low_codes = words % 16  50.3 us
    select_n x1, local copies, waits for them, and re-layouts, unpack(): high_codes = words // 16  49.1 us
    select_n x1, local copies, waits for them, and re-layouts, unpack(): low_codes = words % 16  48.9 us
    sub x1, local copies, waits for them, and re-layouts, unpack(): codes.reshape(groups, GROUP, 2 * half_cols) - zero_rows[:, None, :]  34.2 us
    mul x1, local copies, waits for them, and re-layouts, unpack(): shifted * scale_rows[:, None, :]  31.7 us
  transfers between devices with their start and end apart: 3, of which 1 were waited for; matrix products, arithmetic and copies ran while one was open for 89% of the time, Pallas kernels for 0%

commit v1 on v0

v1 whole, which is shorter than its diff:
```python
import jax
import jax.numpy as jnp
from jax import lax
from jax.experimental import pallas as pl
from jax.experimental.pallas import tpu as pltpu
from jax.sharding import PartitionSpec as P

GROUP = 128
HALF = 128
ROWS = 16
CHUNK = 64
TILE = 256
MESH = pl.DeviceIdType.MESH

adapter_gain = 0.5

CHAINS = {16: (4, 2, 2), 64: (4, 8, 2)}
ORDERS = ((2, 0, 1), (1, 0, 2), (0, 2, 1), (0, 1, 2))


def chain_place(me, i, n):
    lower = 2 * me < n
    low = jnp.where(lower, me, n - 1 - me)
    near = jnp.where(lax.rem(i, 2) == 1, low - lax.div(i + 1, 2), low + lax.div(i, 2))
    place = jnp.where(i <= 2 * low, near, i)
    return jnp.where(lower, place, n - 1 - place)


def earlier(d, e, q, pieces):
    yes = None
    for k in range(min(pieces, len(ORDERS))):
        if ORDERS[k].index(d) < ORDERS[k].index(e):
            hit = lax.rem(q, len(ORDERS)) == k
            yes = hit if yes is None else jnp.logical_or(yes, hit)
    return yes


def sends_per_place(e, chains, pieces):
    total = 0
    for q in range(pieces):
        order = ORDERS[q % len(ORDERS)]
        count = 1
        for d in order[: order.index(e)]:
            count *= chains[d]
        total += count
    return total


def kernel(
    chains, cores, pieces,
    own_ref, codes_ref, zero_ref, scale_ref, divisor_ref, down_ref, up_ref,
    inbox_ref, gathered_ref,
    weight, grads, words, stage, inner, zeros, scales,
    recv_sems, send_sems, own_sem, grads_sem, words_sems, stage_sems, inbox_sems,
):
    wide, core = lax.axis_index("wide"), lax.axis_index("narrow")
    n0, n1, n2 = chains
    strides = (n1 * n2, n2, 1)
    here = (lax.div(wide, n1 * n2), lax.rem(lax.div(wide, n2), n1), lax.rem(wide, n2))
    channels, columns = weight.shape
    plane_pieces = n1 * n2 * pieces
    plane_rows = plane_pieces * ROWS
    own_rows = inbox_ref.shape[1]
    block_rows = min(plane_rows, own_rows)
    blocks = plane_rows // block_rows
    chunks = channels // CHUNK
    tiles = channels // TILE

    def load_words(c, slot):
        return pltpu.make_async_copy(
            codes_ref.at[pl.ds(pl.multiple_of(c * CHUNK, CHUNK), CHUNK), :],
            words.at[slot],
            words_sems.at[slot],
        )

    own_copy = pltpu.make_async_copy(
        own_ref, gathered_ref.at[pl.ds(wide * pieces, pieces)], own_sem
    )
    load_words(0, 0).start()
    own_copy.start()

    barrier = pltpu.get_barrier_semaphore()
    for p in range(1, cores):
        pl.semaphore_signal(
            barrier, inc=1, device_id=(wide, lax.rem(core + p, cores)), device_id_type=MESH
        )
    for e in range(3):
        for step in (1, -1):
            @pl.when((here[e] + step >= 0) & (here[e] + step < chains[e]))
            def _():
                pl.semaphore_signal(
                    barrier, inc=1, device_id=(wide + step * strides[e], core), device_id_type=MESH
                )
    greeted = cores - 1
    for e in range(3):
        greeted = greeted + jnp.where(here[e] > 0, 1, 0) + jnp.where(here[e] < chains[e] - 1, 1, 0)
    pl.semaphore_wait(barrier, greeted)

    def forward(src, index, q, offsets, source):
        for e in range(3):
            if chains[e] == 1:
                continue
            clear = jnp.bool_(True)
            for d in range(3):
                if d != e:
                    met = offsets[d] == 0
                    before = earlier(d, e, q, pieces)
                    clear = clear & (met if before is None else met | before)

            def send(ok, step, sem):
                @pl.when(ok)
                def _():
                    pltpu.make_async_remote_copy(
                        src_ref=src,
                        dst_ref=gathered_ref.at[index],
                        send_sem=send_sems.at[sem],
                        recv_sem=recv_sems.at[index],
                        device_id=(wide + step * strides[e], core),
                        device_id_type=MESH,
                    ).start()

            if chains[e] == 2:
                send(clear & (offsets[e] == 0), 1 - 2 * here[e], 2 * e)
            else:
                send(clear & (source[e] <= here[e]) & (here[e] + 1 < chains[e]), 1, 2 * e)
                send(clear & (source[e] >= here[e]) & (here[e] > 0), -1, 2 * e + 1)

    def start_own(q, _):
        forward(own_ref.at[q], wide * pieces + q, q, (0, 0, 0), here)
        return 0

    lax.fori_loop(0, pieces, start_own, 0)

    def receive(plane, event):
        place, q = lax.div(event, pieces), lax.rem(event, pieces)
        offsets = (plane, lax.div(place, n2), lax.rem(place, n2))
        source = tuple(chain_place(here[d], offsets[d], chains[d]) for d in range(3))
        index = (source[0] * strides[0] + source[1] * strides[1] + source[2]) * pieces + q
        slot = gathered_ref.at[index]
        pltpu.make_async_copy(slot, slot, recv_sems.at[index]).wait()
        forward(slot, index, q, offsets, source)

    def receive_range(plane, low, high):
        def body(event, _):
            receive(plane, event)
            return 0

        lax.fori_loop(low, high, body, 0)

    for k in range(zero_ref.shape[0]):
        zeros[k] = zero_ref[k : k + 1, :].astype(jnp.float32)
        scales[k] = scale_ref[k : k + 1, :]

    first_events = plane_pieces - pieces

    def unpack(c, _):
        slot = lax.rem(c, 2)

        @pl.when(c + 1 < chunks)
        def _():
            load_words(c + 1, 1 - slot).start()

        receive_range(
            0,
            pieces + lax.div(c * first_events, chunks),
            pieces + lax.div((c + 1) * first_events, chunks),
        )
        load_words(c, slot).wait()
        group = lax.div(c * CHUNK, GROUP)
        rows = pl.ds(pl.multiple_of(c * CHUNK, CHUNK), CHUNK)

        def block(b, _):
            packed = words[slot, :, pl.ds(pl.multiple_of(b * HALF, HALF), HALF)]
            for half, codes in enumerate((packed & 15, packed >> 4)):
                at = pl.ds(pl.multiple_of(b * 2 * HALF + half * HALF, HALF), HALF)
                shifted = codes.astype(jnp.float32) - zeros[group, :, at]
                weight[rows, at] = (shifted * scales[group, :, at]).astype(jnp.bfloat16)
            return 0

        lax.fori_loop(0, columns // (2 * HALF), block, 0, unroll=4)
        return 0

    lax.fori_loop(0, chunks, unpack, 0)
    own_copy.wait()

    def stage_done(slot):
        for b in range(blocks):
            part = stage.at[slot, pl.ds(b * block_rows, block_rows)]
            pltpu.make_async_copy(part, part, stage_sems.at[slot, b]).wait()

    def plane_body(g, _):
        plane = chain_place(here[0], g, n0)
        load = pltpu.make_async_copy(
            gathered_ref.at[pl.ds(plane * plane_pieces, plane_pieces)], grads, grads_sem
        )
        load.start()
        load.wait()
        up = up_ref[...]
        sums = lax.dot_general(
            grads[...].reshape(plane_rows, columns),
            jnp.concatenate([up, up], axis=0),
            (((1,), (1,)), ((), ())),
            preferred_element_type=jnp.float32,
        )
        high = sums.astype(jnp.bfloat16)
        rest = (sums - high.astype(jnp.float32)).astype(jnp.bfloat16)
        rank = up_ref.shape[0]
        lane = lax.broadcasted_iota(jnp.int32, sums.shape, 1)
        inner[...] = jnp.where(lane < rank, high.astype(jnp.float32), rest.astype(jnp.float32)).astype(jnp.bfloat16)
        events = jnp.where(g + 1 < n0, plane_pieces, 0)

        def tile_body(j, _):
            receive_range(g + 1, lax.div(j * events, tiles), lax.div((j + 1) * events, tiles))
            count = g * tiles + j
            slot = lax.rem(count, 2)
            at = pl.ds(pl.multiple_of(j * TILE, TILE), TILE)
            main = lax.dot_general(
                grads[...].reshape(plane_rows, columns),
                weight[at, :],
                (((1,), (1,)), ((), ())),
                preferred_element_type=jnp.float32,
            )
            down = down_ref[:, at]
            extra = jnp.dot(
                inner[...], jnp.concatenate([down, down], axis=0), preferred_element_type=jnp.float32
            )

            @pl.when(count >= 2)
            def _():
                stage_done(slot)

            stage[slot] = (main * (1.0 / divisor_ref[:, at]) + adapter_gain * extra).astype(jnp.bfloat16)
            for b in range(blocks):
                row = plane * plane_rows + b * block_rows
                owner = lax.div(row, own_rows)
                src = stage.at[slot, pl.ds(b * block_rows, block_rows)]
                to = pl.ds(pl.multiple_of(lax.rem(row, own_rows), block_rows), block_rows)
                dst = inbox_ref.at[core, to, at]

                @pl.when(owner == core)
                def _():
                    pltpu.make_async_copy(src, dst, stage_sems.at[slot, b]).start()

                @pl.when(owner != core)
                def _():
                    pltpu.make_async_remote_copy(
                        src_ref=src,
                        dst_ref=dst,
                        send_sem=stage_sems.at[slot, b],
                        recv_sem=inbox_sems.at[core],
                        device_id=(wide, owner),
                        device_id_type=MESH,
                    ).start()
            return 0

        lax.fori_loop(0, tiles, tile_body, 0)
        return 0

    lax.fori_loop(0, n0, plane_body, 0)

    stage_done((n0 * tiles - 2) % 2)
    stage_done((n0 * tiles - 1) % 2)
    for p in range(1, cores):
        sender = lax.rem(core + p, cores)
        part = inbox_ref.at[sender]
        pltpu.make_async_copy(part, part, inbox_sems.at[sender]).wait()

    def sent(count, sem):
        part = gathered_ref.at[pl.ds(0, count)]
        pltpu.make_async_copy(part, part, send_sems.at[sem]).wait()

    for e in range(3):
        each = sends_per_place(e, chains, pieces)
        if chains[e] == 2:
            sent(each, 2 * e)
        elif chains[e] > 2:
            for v in range(chains[e]):
                @pl.when(here[e] == v)
                def _():
                    if v + 1 < chains[e]:
                        sent(each * (v + 1), 2 * e)
                    if v > 0:
                        sent(each * (chains[e] - v), 2 * e + 1)


def shards(
    output_gradient,
    packed_weight_codes,
    group_zero_offsets,
    group_scale_table,
    channel_aware_scale,
    adapter_down_matrix,
    adapter_up_matrix,
):
    wide, cores = lax.axis_size("wide"), lax.axis_size("narrow")
    chains = CHAINS.get(wide, (wide, 1, 1))
    rows, columns = output_gradient.shape
    channels = packed_weight_codes.shape[0]
    rank = adapter_up_matrix.shape[0]
    groups = group_scale_table.shape[0]
    pieces = rows // ROWS
    tokens = rows * wide
    own_rows = tokens // cores
    plane_pieces = chains[1] * chains[2] * pieces
    plane_rows = plane_pieces * ROWS
    blocks = plane_rows // min(plane_rows, own_rows)
    dma = pltpu.SemaphoreType.DMA
    any_spec = pl.BlockSpec(memory_space=pl.ANY)
    vmem_spec = pl.BlockSpec(memory_space=pltpu.VMEM)

    def call(*args):
        return kernel(chains, cores, pieces, *args)

    inbox, _ = pl.pallas_call(
        call,
        out_shape=[
            jax.ShapeDtypeStruct((cores, own_rows, channels), jnp.bfloat16),
            jax.ShapeDtypeStruct((wide * pieces, ROWS, columns), jnp.bfloat16),
        ],
        in_specs=[any_spec, any_spec] + [vmem_spec] * 5,
        out_specs=[any_spec, any_spec],
        scratch_shapes=[
            pltpu.VMEM((channels, columns), jnp.bfloat16),
            pltpu.VMEM((plane_pieces, ROWS, columns), jnp.bfloat16),
            pltpu.VMEM((2, CHUNK, columns // 2), jnp.int32),
            pltpu.VMEM((2, plane_rows, TILE), jnp.bfloat16),
            pltpu.VMEM((plane_rows, 2 * rank), jnp.bfloat16),
            pltpu.VMEM((groups, 1, columns), jnp.float32),
            pltpu.VMEM((groups, 1, columns), jnp.float32),
            dma((wide * pieces,)),
            dma((6,)),
            dma,
            dma,
            dma((2,)),
            dma((2, blocks)),
            dma((cores,)),
        ],
        compiler_params=pltpu.CompilerParams(
            collective_id=0, has_side_effects=True, vmem_limit_bytes=60 * 1024 * 1024
        ),
        cost_estimate=pl.CostEstimate(
            flops=2 * tokens * columns * channels,
            bytes_accessed=2 * channels * columns + 6 * tokens * columns,
            transcendentals=0,
        ),
        name="gather_unpack_multiply",
    )(
        output_gradient.reshape(pieces, ROWS, columns),
        packed_weight_codes,
        group_zero_offsets,
        group_scale_table,
        channel_aware_scale.reshape(1, channels),
        adapter_down_matrix.T,
        adapter_up_matrix,
    )
    return jnp.sum(inbox.astype(jnp.float32), axis=0).astype(jnp.bfloat16)


def solution(mesh):
    placed = (
        P("wide", "narrow"),
        P("wide", "narrow"),
        P("wide", "narrow"),
        P("wide", "narrow"),
        P("wide"),
        P("wide", None),
        P(None, "narrow"),
    )
    return jax.shard_map(
        shards, mesh=mesh, in_specs=placed, out_specs=P("narrow", "wide"), check_vma=False
    )
```

time: 524 us -> 211 us (0.40)
  other arithmetic: 234 us -> 6.72 us
  Pallas kernels: 0 us -> 204 us
  local copies, waits for them, and re-layouts: 172 us -> 0 us
  matrix products: 77.2 us -> 0 us
  waiting for transfers between devices: 26.2 us -> 0 us
  between operations: 13.2 us -> 0.01 us
    pallas_call x0 -> x1, Pallas kernels: none -> 204 us  [shards(): pl.pallas_call(call, out_shape=[jax.ShapeDtypeStruct((cores, own_rows, ch...]
    convert_element_type x1 -> x0, other arithmetic: 119 us -> none  [unpack(): (shifted * scale_rows[:, None, :]).reshape(rows, 2 * half_cols)]
    select_n x2 -> x0, local copies, waits for them, and re-layouts: 98 us -> none  [the longest x1 49.1 us: unpack(): high_codes = words // 16]
    dot_general x3 -> x0, matrix products: 77.2 us -> none  [the longest x1 63.1 us: shards(): jnp.einsum('td,kd->tk', collected_rows, weight, preferred_element_type=jn...]
    another operation x1 -> x0, other arithmetic: 65.3 us -> none  [unpack(): jnp.stack([low_codes.reshape(rows, blocks, HALF), high_codes.reshape(rows...]
    select_n x1 -> x0, other arithmetic: 50.3 us -> none  [unpack(): low_codes = words % 16]
    sub x1 -> x0, local copies, waits for them, and re-layouts: 34.2 us -> none  [unpack(): codes.reshape(groups, GROUP, 2 * half_cols) - zero_rows[:, None, :]]
    mul x1 -> x0, local copies, waits for them, and re-layouts: 31.7 us -> none  [unpack(): shifted * scale_rows[:, None, :]]
  transfers between devices with their start and end apart: 3 -> 0, of which waited for: 1 -> 0; matrix products, arithmetic and copies ran while one was open for 89% -> 0% of each run, Pallas kernels for 0% -> 0%
where the time goes in v1:
time: 211 us; the launch traced here: 210 us
  Pallas kernels  204 us (97%)
  other arithmetic  6.72 us (3%)
    pallas_call x1, Pallas kernels, shards(): pl.pallas_call(call, out_shape=[jax.ShapeDtypeStruct((cores, own_rows, ch...  204 us
    reduce_sum x1, other arithmetic, shards(): return jnp.sum(inbox.astype(jnp.float32), axis=0).astype(jnp.bfloat16)  6.72 us

profile of v1, /device:TPU:0, one launch (start us, length us, event | category | flops | bytes accessed | tf_op | source)
XLA Modules:
  0.0 210.4 jit_solution(9855805269231496954)
XLA Ops:
  0.0 203.7 %gather_unpack_multiply.1 = (bf16[2,512,3072]{2,1,0:T(8,128)(2,1)}, bf16[64,16,8192]{2,1,0:T(8,128)(2,1)}) custom-call(bf16[4,16,8192]{2,1,0:T(8,128)(2,1)} %bitcast.3, s32[3072,4096]{1,0:T(8,128)} %args_1_.4, s32[24,8192]{1,0:T(8,128)} %args_2_.4, f32[24,8192]{1,0:T(8,128)} %args_3_.4, f32[1,3072]{1,0:T(1,128)} %bitcast.5, bf16[16,3072]{1,0:T(8,128)(2,1)} %bitcast.4, ...), custom_call_target="tpu_custom_call" | custom-call | flops 51539607552 | bytes 100663296 | tf_op jit(solution)/shard_map/gather_unpack_multiply/pallas_call | solution.py:314
  203.7 6.7 %reduce_sum.12 = bf16[512,3072]{1,0:T(8,128)(2,1)} reduce(bf16[2,512,3072]{2,1,0:T(8,128)(2,1)} %get-tuple-element.6, bf16[]{:T(256)} %constant.2.clone.1), dimensions={0}, to_apply=%region_0.0 | reduce | flops 1572864 | bytes 9437186 | tf_op jit(solution)/shard_map/reduce_sum | solution.py:356

commit v2 on v1

--- a/solution.py
+++ b/solution.py
@@ -1,3 +1,5 @@
+import itertools
+
 import jax
 import jax.numpy as jnp
 from jax import lax
@@ -9,6 +11,7 @@
 HALF = 128
 ROWS = 16
 CHUNK = 64
+WORD_SLOTS = 3
 TILE = 256
 MESH = pl.DeviceIdType.MESH
 
@@ -33,6 +36,27 @@
             hit = lax.rem(q, len(ORDERS)) == k
             yes = hit if yes is None else jnp.logical_or(yes, hit)
     return yes
+
+
+def arrivals(chains, pieces):
+    offsets = list(itertools.product(*map(range, chains)))
+    order = sorted(
+        ((place, q) for place in offsets[1:] for q in range(pieces)),
+        key=lambda event: (sum(event[0]), event[1], event[0]),
+    )
+    codes = [offsets.index(place) * pieces + q for place, q in order]
+    cuts = [
+        max([at + 1 for at, (place, _) in enumerate(order) if place[0] <= plane], default=0)
+        for plane in range(chains[0])
+    ]
+    return codes, cuts
+
+
+def pick(values, at):
+    result = jnp.int32(values[0])
+    for k in range(1, len(values)):
+        result = jnp.where(at == k, jnp.int32(values[k]), result)
+    return result
 
 
 def sends_per_place(e, chains, pieces):
@@ -64,6 +88,7 @@
     block_rows = min(plane_rows, own_rows)
     blocks = plane_rows // block_rows
     chunks = channels // CHUNK
+    depth = words.shape[0]
     tiles = channels // TILE
 
     def load_words(c, slot):
@@ -76,7 +101,8 @@
     own_copy = pltpu.make_async_copy(
         own_ref, gathered_ref.at[pl.ds(wide * pieces, pieces)], own_sem
     )
-    load_words(0, 0).start()
+    for c in range(depth - 1):
+        load_words(c, c).start()
     own_copy.start()
 
     barrier = pltpu.get_barrier_semaphore()
@@ -131,40 +157,43 @@
 
     lax.fori_loop(0, pieces, start_own, 0)
 
-    def receive(plane, event):
-        place, q = lax.div(event, pieces), lax.rem(event, pieces)
-        offsets = (plane, lax.div(place, n2), lax.rem(place, n2))
+    codes, cuts = arrivals(chains, pieces)
+    bits = max(1, (n0 * n1 * n2 * pieces - 1).bit_length())
+    per_word = 30 // bits
+    packed_codes = [
+        sum(code << (bits * k) for k, code in enumerate(codes[at : at + per_word]))
+        for at in range(0, len(codes), per_word)
+    ]
+    first = min(len(codes), cuts[0] + len(codes) // 20)
+    done = [max(first, cut) for cut in cuts] + [len(codes)]
+
+    def receive(event, _):
+        word = pick(packed_codes, lax.div(event, per_word))
+        code = (word >> (lax.rem(event, per_word) * bits)) & ((1 << bits) - 1)
+        place, q = lax.div(code, pieces), lax.rem(code, pieces)
+        offsets = (lax.div(place, n1 * n2), lax.rem(lax.div(place, n2), n1), lax.rem(place, n2))
         source = tuple(chain_place(here[d], offsets[d], chains[d]) for d in range(3))
         index = (source[0] * strides[0] + source[1] * strides[1] + source[2]) * pieces + q
         slot = gathered_ref.at[index]
         pltpu.make_async_copy(slot, slot, recv_sems.at[index]).wait()
         forward(slot, index, q, offsets, source)
-
-    def receive_range(plane, low, high):
-        def body(event, _):
-            receive(plane, event)
-            return 0
-
-        lax.fori_loop(low, high, body, 0)
+        return 0
+
+    def receive_range(low, high):
+        lax.fori_loop(low, high, receive, 0)
 
     for k in range(zero_ref.shape[0]):
         zeros[k] = zero_ref[k : k + 1, :].astype(jnp.float32)
         scales[k] = scale_ref[k : k + 1, :]
 
-    first_events = plane_pieces - pieces
-
     def unpack(c, _):
-        slot = lax.rem(c, 2)
-
-        @pl.when(c + 1 < chunks)
+        slot = lax.rem(c, depth)
+
+        @pl.when(c + depth - 1 < chunks)
         def _():
-            load_words(c + 1, 1 - slot).start()
-
-        receive_range(
-            0,
-            pieces + lax.div(c * first_events, chunks),
-            pieces + lax.div((c + 1) * first_events, chunks),
-        )
+            load_words(c + depth - 1, lax.rem(c + depth - 1, depth)).start()
+
+        receive_range(lax.div(c * first, chunks), lax.div((c + 1) * first, chunks))
         load_words(c, slot).wait()
         group = lax.div(c * CHUNK, GROUP)
         rows = pl.ds(pl.multiple_of(c * CHUNK, CHUNK), CHUNK)
@@ -207,10 +236,10 @@
         rank = up_ref.shape[0]
         lane = lax.broadcasted_iota(jnp.int32, sums.shape, 1)
         inner[...] = jnp.where(lane < rank, high.astype(jnp.float32), rest.astype(jnp.float32)).astype(jnp.bfloat16)
-        events = jnp.where(g + 1 < n0, plane_pieces, 0)
+        low, events = pick(done, g), pick(done, g + 1) - pick(done, g)
 
         def tile_body(j, _):
-            receive_range(g + 1, lax.div(j * events, tiles), lax.div((j + 1) * events, tiles))
+            receive_range(low + lax.div(j * events, tiles), low + lax.div((j + 1) * events, tiles))
             count = g * tiles + j
             slot = lax.rem(count, 2)
             at = pl.ds(pl.multiple_of(j * TILE, TILE), TILE)
@@ -322,7 +351,7 @@
         scratch_shapes=[
             pltpu.VMEM((channels, columns), jnp.bfloat16),
             pltpu.VMEM((plane_pieces, ROWS, columns), jnp.bfloat16),
-            pltpu.VMEM((2, CHUNK, columns // 2), jnp.int32),
+            pltpu.VMEM((WORD_SLOTS, CHUNK, columns // 2), jnp.int32),
             pltpu.VMEM((2, plane_rows, TILE), jnp.bfloat16),
             pltpu.VMEM((plane_rows, 2 * rank), jnp.bfloat16),
             pltpu.VMEM((groups, 1, columns), jnp.float32),
@@ -331,7 +360,7 @@
             dma((6,)),
             dma,
             dma,
-            dma((2,)),
+            dma((WORD_SLOTS,)),
             dma((2, blocks)),
             dma((cores,)),
         ],
@@ -353,7 +382,10 @@
         adapter_down_matrix.T,
         adapter_up_matrix,
     )
-    return jnp.sum(inbox.astype(jnp.float32), axis=0).astype(jnp.bfloat16)
+    total = inbox[0].astype(jnp.float32)
+    for p in range(1, cores):
+        total = total + inbox[p].astype(jnp.float32)
+    return total.astype(jnp.bfloat16)
 
 
 def solution(mesh):

time: 211 us -> 167 us (0.79)
  Pallas kernels: 204 us -> 161 us
    pallas_call x1, Pallas kernels: 204 us -> 161 us  [shards(): pl.pallas_call(call, out_shape=[jax.ShapeDtypeStruct((cores, own_rows, ch...]
    reduce_sum x1 -> x0, other arithmetic: 6.72 us -> none  [shards(): return jnp.sum(inbox.astype(jnp.float32), axis=0).astype(jnp.bfloat16)]
    convert_element_type x0 -> x1, other arithmetic: none -> 5.66 us  [shards(): return total.astype(jnp.bfloat16)]
where the time goes in v2:
time: 167 us
  Pallas kernels  161 us (96%)
  other arithmetic  5.66 us (3%)
    pallas_call x1, Pallas kernels, shards(): pl.pallas_call(call, out_shape=[jax.ShapeDtypeStruct((cores, own_rows, ch...  161 us
    convert_element_type x1, other arithmetic, shards(): return total.astype(jnp.bfloat16)  5.66 us

profile of v2, /device:TPU:0, one launch (start us, length us, event | category | flops | bytes accessed | tf_op | source)
XLA Modules:
  0.0 166.9 jit_solution(10576055191134164181)
XLA Ops:
  0.0 161.2 %gather_unpack_multiply.1 = (bf16[2,512,3072]{2,1,0:T(8,128)(2,1)}, bf16[64,16,8192]{2,1,0:T(8,128)(2,1)}) custom-call(bf16[4,16,8192]{2,1,0:T(8,128)(2,1)} %bitcast.5, s32[3072,4096]{1,0:T(8,128)} %args_1_.4, s32[24,8192]{1,0:T(8,128)} %args_2_.4, f32[24,8192]{1,0:T(8,128)} %args_3_.4, f32[1,3072]{1,0:T(1,128)} %bitcast.7, bf16[16,3072]{1,0:T(8,128)(2,1)} %bitcast.6, ...), custom_call_target="tpu_custom_call" | custom-call | flops 51539607552 | bytes 100663296 | tf_op jit(solution)/shard_map/gather_unpack_multiply/pallas_call | solution.py:343
  161.2 5.7 %fusion = bf16[512,3072]{1,0:T(8,128)(2,1)} fusion(bf16[2,512,3072]{2,1,0:T(8,128)(2,1)} %get-tuple-element.6), kind=kLoop, calls=%fused_computation.1 | loop fusion | flops 6291456 | bytes 9437184 | tf_op jit(solution)/shard_map/convert_element_type | solution.py:388

commit v3 on v2

--- a/solution.py
+++ b/solution.py
@@ -12,7 +12,8 @@
 ROWS = 16
 CHUNK = 64
 WORD_SLOTS = 3
-TILE = 256
+TILE = 512
+VMEM_BYTES = 60 * 1024 * 1024 + 512 * 1024
 MESH = pl.DeviceIdType.MESH
 
 adapter_gain = 0.5
@@ -72,10 +73,10 @@
 
 def kernel(
     chains, cores, pieces,
-    own_ref, codes_ref, zero_ref, scale_ref, divisor_ref, down_ref, up_ref,
+    own_ref, codes_ref, zero_hbm, scale_hbm, up_hbm, divisor_ref, down_ref,
     inbox_ref, gathered_ref,
-    weight, grads, words, stage, inner, zeros, scales,
-    recv_sems, send_sems, own_sem, grads_sem, words_sems, stage_sems, inbox_sems,
+    weight, grads, words, stage, inner, zeros, scales, zero_ref, scale_ref, up_ref,
+    recv_sems, send_sems, own_sem, table_sems, grads_sem, words_sems, stage_sems, inbox_sems,
 ):
     wide, core = lax.axis_index("wide"), lax.axis_index("narrow")
     n0, n1, n2 = chains
@@ -89,7 +90,8 @@
     blocks = plane_rows // block_rows
     chunks = channels // CHUNK
     depth = words.shape[0]
-    tiles = channels // TILE
+    tile = stage.shape[2]
+    tiles = channels // tile
 
     def load_words(c, slot):
         return pltpu.make_async_copy(
@@ -104,6 +106,14 @@
     for c in range(depth - 1):
         load_words(c, c).start()
     own_copy.start()
+    tables = [
+        pltpu.make_async_copy(src, dst, table_sems.at[k])
+        for k, (src, dst) in enumerate(
+            ((zero_hbm, zero_ref), (scale_hbm, scale_ref), (up_hbm, up_ref))
+        )
+    ]
+    for table in tables:
+        table.start()
 
     barrier = pltpu.get_barrier_semaphore()
     for p in range(1, cores):
@@ -182,6 +192,8 @@
     def receive_range(low, high):
         lax.fori_loop(low, high, receive, 0)
 
+    for table in tables:
+        table.wait()
     for k in range(zero_ref.shape[0]):
         zeros[k] = zero_ref[k : k + 1, :].astype(jnp.float32)
         scales[k] = scale_ref[k : k + 1, :]
@@ -242,13 +254,13 @@
             receive_range(low + lax.div(j * events, tiles), low + lax.div((j + 1) * events, tiles))
             count = g * tiles + j
             slot = lax.rem(count, 2)
-            at = pl.ds(pl.multiple_of(j * TILE, TILE), TILE)
+            at = pl.ds(pl.multiple_of(j * tile, tile), tile)
             main = lax.dot_general(
+                weight[at, :],
                 grads[...].reshape(plane_rows, columns),
-                weight[at, :],
                 (((1,), (1,)), ((), ())),
                 preferred_element_type=jnp.float32,
-            )
+            ).T
             down = down_ref[:, at]
             extra = jnp.dot(
                 inner[...], jnp.concatenate([down, down], axis=0), preferred_element_type=jnp.float32
@@ -333,6 +345,7 @@
     plane_pieces = chains[1] * chains[2] * pieces
     plane_rows = plane_pieces * ROWS
     blocks = plane_rows // min(plane_rows, own_rows)
+    tile = TILE if channels % TILE == 0 else TILE // 2
     dma = pltpu.SemaphoreType.DMA
     any_spec = pl.BlockSpec(memory_space=pl.ANY)
     vmem_spec = pl.BlockSpec(memory_space=pltpu.VMEM)
@@ -346,26 +359,30 @@
             jax.ShapeDtypeStruct((cores, own_rows, channels), jnp.bfloat16),
             jax.ShapeDtypeStruct((wide * pieces, ROWS, columns), jnp.bfloat16),
         ],
-        in_specs=[any_spec, any_spec] + [vmem_spec] * 5,
+        in_specs=[any_spec] * 5 + [vmem_spec] * 2,
         out_specs=[any_spec, any_spec],
         scratch_shapes=[
             pltpu.VMEM((channels, columns), jnp.bfloat16),
             pltpu.VMEM((plane_pieces, ROWS, columns), jnp.bfloat16),
             pltpu.VMEM((WORD_SLOTS, CHUNK, columns // 2), jnp.int32),
-            pltpu.VMEM((2, plane_rows, TILE), jnp.bfloat16),
+            pltpu.VMEM((2, plane_rows, tile), jnp.bfloat16),
             pltpu.VMEM((plane_rows, 2 * rank), jnp.bfloat16),
             pltpu.VMEM((groups, 1, columns), jnp.float32),
             pltpu.VMEM((groups, 1, columns), jnp.float32),
+            pltpu.VMEM((groups, columns), jnp.int32),
+            pltpu.VMEM((groups, columns), jnp.float32),
+            pltpu.VMEM((rank, columns), jnp.bfloat16),
             dma((wide * pieces,)),
             dma((6,)),
             dma,
+            dma((3,)),
             dma,
             dma((WORD_SLOTS,)),
             dma((2, blocks)),
             dma((cores,)),
         ],
         compiler_params=pltpu.CompilerParams(
-            collective_id=0, has_side_effects=True, vmem_limit_bytes=60 * 1024 * 1024
+            collective_id=0, has_side_effects=True, vmem_limit_bytes=VMEM_BYTES
         ),
         cost_estimate=pl.CostEstimate(
             flops=2 * tokens * columns * channels,
@@ -378,14 +395,37 @@
         packed_weight_codes,
         group_zero_offsets,
         group_scale_table,
+        adapter_up_matrix,
         channel_aware_scale.reshape(1, channels),
         adapter_down_matrix.T,
-        adapter_up_matrix,
     )
-    total = inbox[0].astype(jnp.float32)
-    for p in range(1, cores):
-        total = total + inbox[p].astype(jnp.float32)
-    return total.astype(jnp.bfloat16)
+    return add_slots(inbox)
+
+
+def add_slots(inbox):
+    cores, rows, channels = inbox.shape
+    block = min(64, rows)
+
+    def body(inbox_ref, out_ref):
+        total = inbox_ref[0].astype(jnp.float32)
+        for p in range(1, cores):
+            total = total + inbox_ref[p].astype(jnp.float32)
+        out_ref[...] = total.astype(jnp.bfloat16)
+
+    return pl.pallas_call(
+        body,
+        out_shape=jax.ShapeDtypeStruct((rows, channels), jnp.bfloat16),
+        grid=(rows // block,),
+        in_specs=[pl.BlockSpec((cores, block, channels), lambda i: (0, i, 0))],
+        out_specs=pl.BlockSpec((block, channels), lambda i: (i, 0)),
+        compiler_params=pltpu.CompilerParams(vmem_limit_bytes=32 * 1024 * 1024),
+        cost_estimate=pl.CostEstimate(
+            flops=cores * rows * channels,
+            bytes_accessed=2 * (cores + 1) * rows * channels,
+            transcendentals=0,
+        ),
+        name="add_slots",
+    )(inbox)
 
 
 def solution(mesh):

time: 167 us -> 166 us (level)
  other arithmetic: 5.66 us -> 0 us
  local copies, waits for them, and re-layouts: 0 us -> 2.78 us
    convert_element_type x1 -> x0, other arithmetic: 5.66 us -> none  [shards(): return total.astype(jnp.bfloat16)]
    pallas_call x0 -> x1, Pallas kernels: none -> 3.75 us  [add_slots(): pl.pallas_call(body, out_shape=jax.ShapeDtypeStruct((rows, channels), jnp...]
    unnamed x0 -> x2, local copies, waits for them, and re-layouts: none -> 2.78 us
    pallas_call x1, Pallas kernels: 161 us -> 159 us  [shards(): pl.pallas_call(call, out_shape=[jax.ShapeDtypeStruct((cores, own_rows, ch...]
where the time goes in v3:
time: 166 us; the launch traced here: 165 us
  Pallas kernels  162 us (98%)
  local copies, waits for them, and re-layouts  2.78 us (2%)
    pallas_call x1, Pallas kernels, shards(): pl.pallas_call(call, out_shape=[jax.ShapeDtypeStruct((cores, own_rows, ch...  159 us
    pallas_call x1, Pallas kernels, add_slots(): pl.pallas_call(body, out_shape=jax.ShapeDtypeStruct((rows, channels), jnp...  3.75 us

profile of v3, /device:TPU:0, one launch (start us, length us, event | category | flops | bytes accessed | tf_op | source)
XLA Modules:
  0.0 165.1 jit_solution(7868360654918287040)
XLA Ops:
  0.0 158.5 %gather_unpack_multiply.1 = (bf16[2,512,3072]{2,1,0:T(8,128)(2,1)}, bf16[64,16,8192]{2,1,0:T(8,128)(2,1)}) custom-call(bf16[4,16,8192]{2,1,0:T(8,128)(2,1)} %bitcast.3, s32[3072,4096]{1,0:T(8,128)} %args_1_.4, s32[24,8192]{1,0:T(8,128)} %args_2_.4, f32[24,8192]{1,0:T(8,128)} %args_3_.4, bf16[16,8192]{1,0:T(8,128)(2,1)} %args_4_.4, f32[1,3072]{1,0:T(1,128)} %bitcast.5, ...), custom_call_target="tpu_custom_call" | custom-call | flops 51539607552 | bytes 100663296 | tf_op jit(solution)/shard_map/gather_unpack_multiply/pallas_call | solution.py:356
  158.6 0.0 copy-start
  158.6 2.8 %copy-done = bf16[2,512,3072]{2,1,0:T(8,128)(2,1)S(1)} copy-done((bf16[2,512,3072]{2,1,0:T(8,128)(2,1)S(1)}, bf16[2,512,3072]{2,1,0:T(8,128)(2,1)}, u32[]{:S(2)}) %copy-start) | copy-done | bytes 6291480
  161.3 3.7 %add_slots.1 = bf16[512,3072]{1,0:T(8,128)(2,1)} custom-call(bf16[2,512,3072]{2,1,0:T(8,128)(2,1)S(1)} %copy-done), custom_call_target="tpu_custom_call" | custom-call | flops 3145728 | bytes 9437184 | tf_op jit(solution)/shard_map/add_slots/pallas_call | solution.py:415
Async XLA Ops:
  158.6 2.8 %copy-start = (bf16[2,512,3072]{2,1,0:T(8,128)(2,1)S(1)}, bf16[2,512,3072]{2,1,0:T(8,128)(2,1)}, u32[]{:S(2)}) copy-start(bf16[2,512,3072]{2,1,0:T(8,128)(2,1)} %get-tuple-element.6.inbox_ref) | copy-start | bytes 18874372

commit v4 on v3

--- a/solution.py
+++ b/solution.py
@@ -75,8 +75,8 @@
     chains, cores, pieces,
     own_ref, codes_ref, zero_hbm, scale_hbm, up_hbm, divisor_ref, down_ref,
     inbox_ref, gathered_ref,
-    weight, grads, words, stage, inner, zeros, scales, zero_ref, scale_ref, up_ref,
-    recv_sems, send_sems, own_sem, table_sems, grads_sem, words_sems, stage_sems, inbox_sems,
+    weight, stage, inner, up_ref,
+    recv_sems, send_sems, own_sem, table_sems, grads_sems, words_sems, stage_sems, inbox_sems,
 ):
     wide, core = lax.axis_index("wide"), lax.axis_index("narrow")
     n0, n1, n2 = chains
@@ -89,48 +89,30 @@
     block_rows = min(plane_rows, own_rows)
     blocks = plane_rows // block_rows
     chunks = channels // CHUNK
-    depth = words.shape[0]
     tile = stage.shape[2]
     tiles = channels // tile
 
-    def load_words(c, slot):
-        return pltpu.make_async_copy(
-            codes_ref.at[pl.ds(pl.multiple_of(c * CHUNK, CHUNK), CHUNK), :],
-            words.at[slot],
-            words_sems.at[slot],
-        )
-
     own_copy = pltpu.make_async_copy(
         own_ref, gathered_ref.at[pl.ds(wide * pieces, pieces)], own_sem
     )
-    for c in range(depth - 1):
-        load_words(c, c).start()
-    own_copy.start()
-    tables = [
-        pltpu.make_async_copy(src, dst, table_sems.at[k])
-        for k, (src, dst) in enumerate(
-            ((zero_hbm, zero_ref), (scale_hbm, scale_ref), (up_hbm, up_ref))
-        )
-    ]
-    for table in tables:
-        table.start()
-
-    barrier = pltpu.get_barrier_semaphore()
-    for p in range(1, cores):
-        pl.semaphore_signal(
-            barrier, inc=1, device_id=(wide, lax.rem(core + p, cores)), device_id_type=MESH
-        )
-    for e in range(3):
-        for step in (1, -1):
-            @pl.when((here[e] + step >= 0) & (here[e] + step < chains[e]))
-            def _():
-                pl.semaphore_signal(
-                    barrier, inc=1, device_id=(wide + step * strides[e], core), device_id_type=MESH
-                )
-    greeted = cores - 1
-    for e in range(3):
-        greeted = greeted + jnp.where(here[e] > 0, 1, 0) + jnp.where(here[e] < chains[e] - 1, 1, 0)
-    pl.semaphore_wait(barrier, greeted)
+
+    def greet():
+        barrier = pltpu.get_barrier_semaphore()
+        for p in range(1, cores):
+            pl.semaphore_signal(
+                barrier, inc=1, device_id=(wide, lax.rem(core + p, cores)), device_id_type=MESH
+            )
+        for e in range(3):
+            for step in (1, -1):
+                @pl.when((here[e] + step >= 0) & (here[e] + step < chains[e]))
+                def _():
+                    pl.semaphore_signal(
+                        barrier, inc=1, device_id=(wide + step * strides[e], core), device_id_type=MESH
+                    )
+        greeted = cores - 1
+        for e in range(3):
+            greeted = greeted + jnp.where(here[e] > 0, 1, 0) + jnp.where(here[e] < chains[e] - 1, 1, 0)
+        pl.semaphore_wait(barrier, greeted)
 
     def forward(src, index, q, offsets, source):
         for e in range(3):
@@ -165,8 +147,6 @@
         forward(own_ref.at[q], wide * pieces + q, q, (0, 0, 0), here)
         return 0
 
-    lax.fori_loop(0, pieces, start_own, 0)
-
     codes, cuts = arrivals(chains, pieces)
     bits = max(1, (n0 * n1 * n2 * pieces - 1).bit_length())
     per_word = 30 // bits
@@ -192,36 +172,71 @@
     def receive_range(low, high):
         lax.fori_loop(low, high, receive, 0)
 
-    for table in tables:
-        table.wait()
-    for k in range(zero_ref.shape[0]):
-        zeros[k] = zero_ref[k : k + 1, :].astype(jnp.float32)
-        scales[k] = scale_ref[k : k + 1, :]
-
-    def unpack(c, _):
-        slot = lax.rem(c, depth)
-
-        @pl.when(c + depth - 1 < chunks)
-        def _():
-            load_words(c + depth - 1, lax.rem(c + depth - 1, depth)).start()
-
-        receive_range(lax.div(c * first, chunks), lax.div((c + 1) * first, chunks))
-        load_words(c, slot).wait()
-        group = lax.div(c * CHUNK, GROUP)
-        rows = pl.ds(pl.multiple_of(c * CHUNK, CHUNK), CHUNK)
-
-        def block(b, _):
-            packed = words[slot, :, pl.ds(pl.multiple_of(b * HALF, HALF), HALF)]
-            for half, codes in enumerate((packed & 15, packed >> 4)):
-                at = pl.ds(pl.multiple_of(b * 2 * HALF + half * HALF, HALF), HALF)
-                shifted = codes.astype(jnp.float32) - zeros[group, :, at]
-                weight[rows, at] = (shifted * scales[group, :, at]).astype(jnp.bfloat16)
+    def unpack_all(words, zeros, scales, zero_ref, scale_ref):
+        depth = words.shape[0]
+
+        def load_words(c, slot):
+            return pltpu.make_async_copy(
+                codes_ref.at[pl.ds(pl.multiple_of(c * CHUNK, CHUNK), CHUNK), :],
+                words.at[slot],
+                words_sems.at[slot],
+            )
+
+        for c in range(depth - 1):
+            load_words(c, c).start()
+        own_copy.start()
+        tables = [
+            pltpu.make_async_copy(src, dst, table_sems.at[k])
+            for k, (src, dst) in enumerate(
+                ((zero_hbm, zero_ref), (scale_hbm, scale_ref), (up_hbm, up_ref))
+            )
+        ]
+        for table in tables:
+            table.start()
+
+        greet()
+        lax.fori_loop(0, pieces, start_own, 0)
+
+        for table in tables:
+            table.wait()
+        for k in range(zero_ref.shape[0]):
+            zeros[k] = zero_ref[k : k + 1, :].astype(jnp.float32)
+            scales[k] = scale_ref[k : k + 1, :]
+
+        def unpack(c, _):
+            slot = lax.rem(c, depth)
+
+            @pl.when(c + depth - 1 < chunks)
+            def _():
+                load_words(c + depth - 1, lax.rem(c + depth - 1, depth)).start()
+
+            receive_range(lax.div(c * first, chunks), lax.div((c + 1) * first, chunks))
+            load_words(c, slot).wait()
+            group = lax.div(c * CHUNK, GROUP)
+            rows = pl.ds(pl.multiple_of(c * CHUNK, CHUNK), CHUNK)
+
+            def block(b, _):
+                packed = words[slot, :, pl.ds(pl.multiple_of(b * HALF, HALF), HALF)]
+                for half, codes in enumerate((packed & 15, packed >> 4)):
+                    at = pl.ds(pl.multiple_of(b * 2 * HALF + half * HALF, HALF), HALF)
+                    shifted = codes.astype(jnp.float32) - zeros[group, :, at]
+                    weight[rows, at] = (shifted * scales[group, :, at]).astype(jnp.bfloat16)
+                return 0
+
+            lax.fori_loop(0, columns // (2 * HALF), block, 0, unroll=4)
             return 0
 
-        lax.fori_loop(0, columns // (2 * HALF), block, 0, unroll=4)
-        return 0
-
-    lax.fori_loop(0, chunks, unpack, 0)
+        lax.fori_loop(0, chunks, unpack, 0)
+
+    groups = zero_hbm.shape[0]
+    pl.run_scoped(
+        unpack_all,
+        pltpu.VMEM((WORD_SLOTS, CHUNK, columns // 2), jnp.int32),
+        pltpu.VMEM((groups, 1, columns), jnp.float32),
+        pltpu.VMEM((groups, 1, columns), jnp.float32),
+        pltpu.VMEM((groups, columns), jnp.int32),
+        pltpu.VMEM((groups, columns), jnp.float32),
+    )
     own_copy.wait()
 
     def stage_done(slot):
@@ -229,75 +244,89 @@
             part = stage.at[slot, pl.ds(b * block_rows, block_rows)]
             pltpu.make_async_copy(part, part, stage_sems.at[slot, b]).wait()
 
-    def plane_body(g, _):
-        plane = chain_place(here[0], g, n0)
-        load = pltpu.make_async_copy(
-            gathered_ref.at[pl.ds(plane * plane_pieces, plane_pieces)], grads, grads_sem
-        )
-        load.start()
-        load.wait()
-        up = up_ref[...]
-        sums = lax.dot_general(
-            grads[...].reshape(plane_rows, columns),
-            jnp.concatenate([up, up], axis=0),
-            (((1,), (1,)), ((), ())),
-            preferred_element_type=jnp.float32,
-        )
-        high = sums.astype(jnp.bfloat16)
-        rest = (sums - high.astype(jnp.float32)).astype(jnp.bfloat16)
-        rank = up_ref.shape[0]
-        lane = lax.broadcasted_iota(jnp.int32, sums.shape, 1)
-        inner[...] = jnp.where(lane < rank, high.astype(jnp.float32), rest.astype(jnp.float32)).astype(jnp.bfloat16)
-        low, events = pick(done, g), pick(done, g + 1) - pick(done, g)
-
-        def tile_body(j, _):
-            receive_range(low + lax.div(j * events, tiles), low + lax.div((j + 1) * events, tiles))
-            count = g * tiles + j
-            slot = lax.rem(count, 2)
-            at = pl.ds(pl.multiple_of(j * tile, tile), tile)
-            main = lax.dot_general(
-                weight[at, :],
-                grads[...].reshape(plane_rows, columns),
+    def multiply_all(grads):
+        def load_plane(g):
+            plane = chain_place(here[0], g, n0)
+            return pltpu.make_async_copy(
+                gathered_ref.at[pl.ds(plane * plane_pieces, plane_pieces)],
+                grads.at[lax.rem(g, 2)],
+                grads_sems.at[lax.rem(g, 2)],
+            )
+
+        def plane_body(g, _):
+            plane = chain_place(here[0], g, n0)
+            held = lax.rem(g, 2)
+            load_plane(g).wait()
+            up = up_ref[...]
+            sums = lax.dot_general(
+                grads[held].reshape(plane_rows, columns),
+                jnp.concatenate([up, up], axis=0),
                 (((1,), (1,)), ((), ())),
                 preferred_element_type=jnp.float32,
-            ).T
-            down = down_ref[:, at]
-            extra = jnp.dot(
-                inner[...], jnp.concatenate([down, down], axis=0), preferred_element_type=jnp.float32
             )
-
-            @pl.when(count >= 2)
-            def _():
-                stage_done(slot)
-
-            stage[slot] = (main * (1.0 / divisor_ref[:, at]) + adapter_gain * extra).astype(jnp.bfloat16)
-            for b in range(blocks):
-                row = plane * plane_rows + b * block_rows
-                owner = lax.div(row, own_rows)
-                src = stage.at[slot, pl.ds(b * block_rows, block_rows)]
-                to = pl.ds(pl.multiple_of(lax.rem(row, own_rows), block_rows), block_rows)
-                dst = inbox_ref.at[core, to, at]
-
-                @pl.when(owner == core)
+            high = sums.astype(jnp.bfloat16)
+            rest = (sums - high.astype(jnp.float32)).astype(jnp.bfloat16)
+            rank = up_ref.shape[0]
+            lane = lax.broadcasted_iota(jnp.int32, sums.shape, 1)
+            inner[...] = jnp.where(lane < rank, high.astype(jnp.float32), rest.astype(jnp.float32)).astype(jnp.bfloat16)
+            low, events = pick(done, g), pick(done, g + 1) - pick(done, g)
+
+            def tile_body(j, _):
+                receive_range(low + lax.div(j * events, tiles), low + lax.div((j + 1) * events, tiles))
+
+                @pl.when((j == tiles - 1) & (g + 1 < n0))
                 def _():
-                    pltpu.make_async_copy(src, dst, stage_sems.at[slot, b]).start()
-
-                @pl.when(owner != core)
+                    load_plane(g + 1).start()
+
+                count = g * tiles + j
+                slot = lax.rem(count, 2)
+                at = pl.ds(pl.multiple_of(j * tile, tile), tile)
+                main = lax.dot_general(
+                    weight[at, :],
+                    grads[held].reshape(plane_rows, columns),
+                    (((1,), (1,)), ((), ())),
+                    preferred_element_type=jnp.float32,
+                ).T
+                down = down_ref[:, at]
+                extra = jnp.dot(
+                    inner[...], jnp.concatenate([down, down], axis=0), preferred_element_type=jnp.float32
+                )
+
+                @pl.when(count >= 2)
                 def _():
-                    pltpu.make_async_remote_copy(
-                        src_ref=src,
-                        dst_ref=dst,
-                        send_sem=stage_sems.at[slot, b],
-                        recv_sem=inbox_sems.at[core],
-                        device_id=(wide, owner),
-                        device_id_type=MESH,
-                    ).start()
+                    stage_done(slot)
+
+                stage[slot] = (main * (1.0 / divisor_ref[:, at]) + adapter_gain * extra).astype(jnp.bfloat16)
+                for b in range(blocks):
+                    row = plane * plane_rows + b * block_rows
+                    owner = lax.div(row, own_rows)
+                    src = stage.at[slot, pl.ds(b * block_rows, block_rows)]
+                    to = pl.ds(pl.multiple_of(lax.rem(row, own_rows), block_rows), block_rows)
+                    dst = inbox_ref.at[core, to, at]
+
+                    @pl.when(owner == core)
+                    def _():
+                        pltpu.make_async_copy(src, dst, stage_sems.at[slot, b]).start()
+
+                    @pl.when(owner != core)
+                    def _():
+                        pltpu.make_async_remote_copy(
+                            src_ref=src,
+                            dst_ref=dst,
+                            send_sem=stage_sems.at[slot, b],
+                            recv_sem=inbox_sems.at[core],
+                            device_id=(wide, owner),
+                            device_id_type=MESH,
+                        ).start()
+                return 0
+
+            lax.fori_loop(0, tiles, tile_body, 0)
             return 0
 
-        lax.fori_loop(0, tiles, tile_body, 0)
-        return 0
-
-    lax.fori_loop(0, n0, plane_body, 0)
+        load_plane(0).start()
+        lax.fori_loop(0, n0, plane_body, 0)
+
+    pl.run_scoped(multiply_all, pltpu.VMEM((2, plane_pieces, ROWS, columns), jnp.bfloat16))
 
     stage_done((n0 * tiles - 2) % 2)
     stage_done((n0 * tiles - 1) % 2)
@@ -338,7 +367,6 @@
     rows, columns = output_gradient.shape
     channels = packed_weight_codes.shape[0]
     rank = adapter_up_matrix.shape[0]
-    groups = group_scale_table.shape[0]
     pieces = rows // ROWS
     tokens = rows * wide
     own_rows = tokens // cores
@@ -363,20 +391,14 @@
         out_specs=[any_spec, any_spec],
         scratch_shapes=[
             pltpu.VMEM((channels, columns), jnp.bfloat16),
-            pltpu.VMEM((plane_pieces, ROWS, columns), jnp.bfloat16),
-            pltpu.VMEM((WORD_SLOTS, CHUNK, columns // 2), jnp.int32),
             pltpu.VMEM((2, plane_rows, tile), jnp.bfloat16),
             pltpu.VMEM((plane_rows, 2 * rank), jnp.bfloat16),
-            pltpu.VMEM((groups, 1, columns), jnp.float32),
-            pltpu.VMEM((groups, 1, columns), jnp.float32),
-            pltpu.VMEM((groups, columns), jnp.int32),
-            pltpu.VMEM((groups, columns), jnp.float32),
             pltpu.VMEM((rank, columns), jnp.bfloat16),
             dma((wide * pieces,)),
             dma((6,)),
             dma,
             dma((3,)),
-            dma,
+            dma((2,)),
             dma((WORD_SLOTS,)),
             dma((2, blocks)),
             dma((cores,)),
@@ -418,7 +440,7 @@
         grid=(rows // block,),
         in_specs=[pl.BlockSpec((cores, block, channels), lambda i: (0, i, 0))],
         out_specs=pl.BlockSpec((block, channels), lambda i: (i, 0)),
-        compiler_params=pltpu.CompilerParams(vmem_limit_bytes=32 * 1024 * 1024),
+        compiler_params=pltpu.CompilerParams(vmem_limit_bytes=VMEM_BYTES),
         cost_estimate=pl.CostEstimate(
             flops=cores * rows * channels,
             bytes_accessed=2 * (cores + 1) * rows * channels,

time: 166 us -> 162 us (0.976)
  local copies, waits for them, and re-layouts: 2.78 us -> 0 us
    pallas_call x1, Pallas kernels: 159 us -> 154 us  [shards(): pl.pallas_call(call, out_shape=[jax.ShapeDtypeStruct((cores, own_rows, ch...]
    pallas_call x1, Pallas kernels: 3.75 us -> 7.01 us  [add_slots(): pl.pallas_call(body, out_shape=jax.ShapeDtypeStruct((rows, channels), jnp...]
    unnamed x2 -> x0, local copies, waits for them, and re-layouts: 2.78 us -> none
where the time goes in v4:
time: 162 us; the launch traced here: 161 us
  Pallas kernels  161 us (99%)
    pallas_call x1, Pallas kernels, shards(): pl.pallas_call(call, out_shape=[jax.ShapeDtypeStruct((cores, own_rows, ch...  154 us
    pallas_call x1, Pallas kernels, add_slots(): pl.pallas_call(body, out_shape=jax.ShapeDtypeStruct((rows, channels), jnp...  7.01 us

profile of v4, /device:TPU:0, one launch (start us, length us, event | category | flops | bytes accessed | tf_op | source)
XLA Modules:
  0.0 161.0 jit_solution(16338484750030863850)
XLA Ops:
  0.0 154.0 %gather_unpack_multiply.1 = (bf16[2,512,3072]{2,1,0:T(8,128)(2,1)}, bf16[64,16,8192]{2,1,0:T(8,128)(2,1)}) custom-call(bf16[4,16,8192]{2,1,0:T(8,128)(2,1)} %bitcast.3, s32[3072,4096]{1,0:T(8,128)} %args_1_.4, s32[24,8192]{1,0:T(8,128)} %args_2_.4, f32[24,8192]{1,0:T(8,128)} %args_3_.4, bf16[16,8192]{1,0:T(8,128)(2,1)} %args_4_.4, f32[1,3072]{1,0:T(1,128)} %bitcast.5, ...), custom_call_target="tpu_custom_call" | custom-call | flops 51539607552 | bytes 100663296 | tf_op jit(solution)/shard_map/gather_unpack_multiply/pallas_call | solution.py:384
  154.0 7.0 %add_slots.1 = bf16[512,3072]{1,0:T(8,128)(2,1)} custom-call(bf16[2,512,3072]{2,1,0:T(8,128)(2,1)} %get-tuple-element.6.inbox_ref), custom_call_target="tpu_custom_call" | custom-call | flops 3145728 | bytes 9437184 | tf_op jit(solution)/shard_map/add_slots/pallas_call | solution.py:437
